TPU v7x, 32 devices: a whole 2x2x4 slice. The times are simulated.
32 devices in a mesh: dp: 2 (over x), cent: 16 (over z, y, core).
Axes of the slice: x: 2, y: 2, z: 4, core: 2. Of those that a mesh axis runs over, the one named last changes fastest.
Arguments:
- vectors: bfloat16 [512, 1024], P(('dp', 'cent')), may hold values from -16 to 16
- centroids: bfloat16 [65536, 1024], P('cent'), may hold values from -0.1125 to 0.1125
Outputs:
- new_centroids: bfloat16 [65536, 1024], P('cent', 'dp')
- loads: float32 [65536], P('cent')
All inputs are finite; a program needn't handle non-finite values.
Results may differ from a plain program's by a relative error of at most 0.0075.
Values may be sent and summed in bfloat16 or wider, within the bound.
A program may use at most 128 MiB of HBM per device.

v0:
```python
import jax
import jax.numpy as jnp
from jax import lax
from jax.sharding import PartitionSpec as P

softness_scale = 0.1


def on_device(vectors, centroids):
    collected_rows = lax.all_gather(vectors, "cent", axis=0, tiled=True)
    logit_scores = (
        lax.dot_general(
            collected_rows, centroids, (((1,), (1,)), ((), ())), preferred_element_type=jnp.float32
        )
        / softness_scale
    )
    local_peak = jnp.max(logit_scores, axis=1)
    highest = lax.pmax(local_peak, "cent")
    exponent = jnp.exp(logit_scores - highest[:, None])
    summed = lax.psum(jnp.sum(exponent, axis=1), "cent")
    probability = exponent / summed[:, None]
    weights = probability.astype(jnp.bfloat16)
    partial_value = lax.dot_general(
        weights, collected_rows, (((0,), (0,)), ((), ())), preferred_element_type=jnp.float32
    )
    counts = lax.psum(jnp.sum(probability, axis=0), "dp")
    total_rows = vectors.shape[0] * lax.axis_size("dp") * lax.axis_size("cent")
    mass_scale = centroids.shape[0] * lax.axis_size("cent") / total_rows
    loads = counts * mass_scale
    full_width = centroids.shape[1]
    columns = full_width // lax.axis_size("dp")
    offset = lax.axis_index("dp") * columns
    sums = lax.psum(partial_value.astype(jnp.bfloat16), "dp").astype(jnp.float32)
    shifted = centroids.astype(jnp.float32) + sums * mass_scale
    factor = lax.rsqrt(jnp.mean(shifted * shifted, axis=1, keepdims=True) + 1e-06)
    updated = (shifted * factor).astype(jnp.bfloat16)
    new_centroids = lax.dynamic_slice_in_dim(updated, offset, columns, 1)
    return (new_centroids, loads)


def solution(mesh):
    placed = (P(("dp", "cent"), None), P("cent", None))
    return jax.shard_map(
        on_device,
        mesh=mesh,
        in_specs=placed,
        out_specs=(P("cent", "dp"), P("cent")),
        check_vma=False,
    )
```

profile of v0, /device:TPU:0, one launch (start us, length us, event | category | flops | bytes accessed | tf_op | source)
XLA Modules:
  0.0 322.7 jit_solution(2879908501470366100)
XLA Ops:
  7.2 0.0 all-reduce.2.cloned.1.call-start
  7.2 24.8 %all_gather.3 = bf16[256,1024]{1,0:T(8,128)(2,1)S(1)} all-gather(bf16[16,1024]{1,0:T(8,128)(2,1)} %param.2), channel_id=1, replica_groups=mesh['dp'=2,'cent'=16] {'cent'}, dimensions={0}, use_global_device_ids=true | all-gather | bytes 557056 | tf_op jit(solution)/shard_map/all_gather | solution.py:10
  32.0 7.8 %fusion.6 = (f32[256]{0:T(256)S(1)}, f32[256,4096]{1,0:T(8,128)}) fusion(bf16[256,1024]{1,0:T(8,128)(2,1)S(1)} %all_gather.3, bf16[4096,1024]{1,0:T(8,128)(2,1)} %param.3), kind=kOutput, calls=%fused_computation.13 | convolution fusion | flops 2149580544 | bytes 13108224 | tf_op jit(solution)/shard_map/dot_general | solution.py:12
  39.8 29.8 %pmax.7 = f32[256]{0:T(256)S(1)} all-reduce(f32[256]{0:T(256)S(1)} %get-tuple-element.4), channel_id=1, replica_groups=mesh['dp'=2,'cent'=16] {'cent'}, use_global_device_ids=true, to_apply=%region_1.0 | all-reduce | flops 256 | bytes 2048 | tf_op jit(solution)/shard_map/pmax | solution.py:18
  69.6 2.9 fusion.2
  72.5 29.5 %psum.21 = f32[256]{0:T(256)S(1)} all-reduce(f32[256]{0:T(256)S(1)} %fusion.2), channel_id=1, replica_groups=mesh['dp'=2,'cent'=16] {'cent'}, use_global_device_ids=true, to_apply=%region_3.0 | all-reduce | flops 256 | bytes 2048 | tf_op jit(solution)/shard_map/psum | solution.py:20
  102.0 8.1 %convolution_convert_fusion = bf16[4096,1024]{1,0:T(8,128)(2,1)} fusion(bf16[256,1024]{1,0:T(8,128)(2,1)S(1)} %all_gather.3, f32[256,4096]{1,0:T(8,128)} %get-tuple-element.5, f32[256]{0:T(256)S(1)} %psum.21, f32[256]{0:T(256)S(1)} %pmax.7), kind=kOutput, calls=%fused_computation.4 | convolution fusion | flops 2154823680 | bytes 13109248 | tf_op jit(solution)/shard_map/dot_general | solution.py:23
  110.1 0.0 all-reduce.2.cloned.1.call-update
  110.1 3.0 fusion.4
  113.2 8.4 %psum.23 = f32[4096]{0:T(1024)S(1)} all-reduce(f32[4096]{0:T(1024)S(1)} %fusion.4), channel_id=1, replica_groups=mesh['dp'=2,'cent'=16] {'dp'}, use_global_device_ids=true, to_apply=%region_7.0 | all-reduce | flops 4096 | bytes 32768 | tf_op jit(solution)/shard_map/psum | solution.py:26
  121.6 0.6 broadcast_multiply_fusion
  122.2 183.5 %all-reduce.2.cloned.1.call-done = bf16[4096,1024]{1,0:T(8,128)(2,1)} async-done(((bf16[4096,1024]{1,0:T(8,128)(2,1)}), bf16[4096,1024]{1,0:T(8,128)(2,1)}) %all-reduce.2.cloned.1.call-update) | async-done | bytes 8388624 | tf_op jit(solution)/shard_map/psum | solution.py:33
  305.7 7.7 %multiply_reduce_fusion = (f32[4096]{0:T(1024)S(1)}, f32[4096,1024]{1,0:T(8,128)S(1)}) fusion(bf16[4096,1024]{1,0:T(8,128)(2,1)} %all-reduce.2.cloned.1.call-done, bf16[4096,1024]{1,0:T(8,128)(2,1)} %param.3), kind=kLoop, calls=%fused_computation | loop fusion | flops 25161728 | bytes 33570816 | tf_op jit(solution)/shard_map/reduce_sum | solution.py:35
  313.5 2.4 fusion
  (1 shorter events, 0.0 us)
Async XLA Ops:
  7.2 298.6 %all-reduce.2.cloned.1.call-start = ((), (), s32[]{:S(2)}) async-start(), calls=%async_computation | async-start | bytes 16777216 | tf_op jit(solution)/shard_map/psum | solution.py:33
Sparse Core Ops, SparseCore 0:
  110.3 195.4 all-reduce.1
where the time goes:
time: 323 us
  waiting for transfers between devices  184 us (57%)
  blocking collectives  92.5 us (29%)
  other arithmetic  16.6 us (5%)
  matrix products  15.9 us (5%)
  between operations  14.1 us (4%)
    psum x1, waiting for transfers between devices, on_device(): lax.psum(partial_value.astype(jnp.bfloat16), 'dp').astype(jnp.float32)  184 us
    pmax x1, blocking collectives, on_device(): highest = lax.pmax(local_peak, 'cent')  29.8 us
    psum x1, blocking collectives, on_device(): summed = lax.psum(jnp.sum(exponent, axis=1), 'cent')  29.5 us
    all_gather x1, blocking collectives, on_device(): collected_rows = lax.all_gather(vectors, 'cent', axis=0, tiled=True)  24.8 us
    psum x1, blocking collectives, on_device(): counts = lax.psum(jnp.sum(probability, axis=0), 'dp')  8.45 us
    dot_general x1, matrix products, on_device(): lax.dot_general(weights, collected_rows, (((0,), (0,)), ((), ())), prefer...  8.14 us
    dot_general x1, matrix products, on_device(): lax.dot_general(collected_rows, centroids, (((1,), (1,)), ((), ())), pref...  7.77 us
    reduce_sum x1, other arithmetic, on_device(): jnp.mean(shifted * shifted, axis=1, keepdims=True) + 1e-06  7.68 us
  transfers between devices with their start and end apart: 1, of which 1 were waited for; matrix products, arithmetic and copies ran while one was open for 1% of the time, Pallas kernels for 0%

commit v1 on v0

v1 whole, which is shorter than its diff:
```python
import jax
import jax.numpy as jnp
from jax import lax
from jax.sharding import PartitionSpec as P

softness_scale = 0.1


def on_device(vectors, centroids):
    dp = lax.axis_size("dp")
    cent = lax.axis_size("cent")
    total_rows = vectors.shape[0] * dp * cent
    mass_scale = centroids.shape[0] * cent / total_rows
    rows = lax.all_gather(vectors, ("dp", "cent"), axis=0, tiled=True)
    scores = (
        lax.dot_general(
            centroids, rows, (((1,), (1,)), ((), ())), preferred_element_type=jnp.float32
        )
        / softness_scale
    )
    local_peak = jnp.max(scores, axis=0)
    exponent = jnp.exp(scores - local_peak[None, :])
    local_sum = jnp.sum(exponent, axis=0)
    stats = lax.all_gather(jnp.stack([local_peak, local_sum]), "cent", axis=0)
    highest = jnp.max(stats[:, 0], axis=0)
    summed = jnp.sum(stats[:, 1] * jnp.exp(stats[:, 0] - highest[None, :]), axis=0)
    rescale = jnp.exp(local_peak - highest) / summed
    probability = exponent * rescale[None, :]
    weights = probability.astype(jnp.bfloat16)
    loads = jnp.sum(probability, axis=1) * mass_scale
    sums = lax.dot_general(
        weights, rows, (((1,), (0,)), ((), ())), preferred_element_type=jnp.float32
    )
    shifted = centroids.astype(jnp.float32) + sums * mass_scale
    factor = lax.rsqrt(jnp.mean(shifted * shifted, axis=1, keepdims=True) + 1e-06)
    columns = centroids.shape[1] // dp
    own = lax.dynamic_slice_in_dim(shifted, lax.axis_index("dp") * columns, columns, 1)
    return ((own * factor).astype(jnp.bfloat16), loads)


def solution(mesh):
    placed = (P(("dp", "cent"), None), P("cent", None))
    return jax.shard_map(
        on_device,
        mesh=mesh,
        in_specs=placed,
        out_specs=(P("cent", "dp"), P("cent")),
        check_vma=False,
    )
```

time: 323 us -> 131 us (0.41)
  waiting for transfers between devices: 184 us -> 48.8 us
  blocking collectives: 92.5 us -> 20.4 us
  local copies, waits for them, and re-layouts: 0 us -> 17.7 us
  other arithmetic: 16.6 us -> 10.2 us
  matrix products: 15.9 us -> 19.3 us
    psum x1 -> x0, waiting for transfers between devices: 184 us -> none  [on_device(): lax.psum(partial_value.astype(jnp.bfloat16), 'dp').astype(jnp.float32)]
    all_gather x0 -> x1, waiting for transfers between devices: none -> 48.2 us  [on_device(): rows = lax.all_gather(vectors, ('dp', 'cent'), axis=0, tiled=True)]
    psum x2 -> x0, blocking collectives: 37.9 us -> none  [the longest x1 29.5 us: on_device(): summed = lax.psum(jnp.sum(exponent, axis=1), 'cent')]
    pmax x1 -> x0, blocking collectives: 29.8 us -> none  [on_device(): highest = lax.pmax(local_peak, 'cent')]
    unnamed x0 -> x4, local copies, waits for them, and re-layouts: none -> 17.7 us
    reduce_sum x3, other arithmetic: 13.6 us -> 3.2 us  [the longest x1 1.72 us: on_device(): loads = jnp.sum(probability, axis=1) * mass_scale]
    all_gather x1, blocking collectives: 24.8 us -> 20.4 us  [on_device(): stats = lax.all_gather(jnp.stack([local_peak, local_sum]), 'cent', axis=0)]
    convert_element_type x1, other arithmetic: 2.38 us -> 6.29 us  [on_device(): return ((own * factor).astype(jnp.bfloat16), loads)]
  transfers between devices with their start and end apart: 1 -> 1, of which waited for: 1 -> 1; matrix products, arithmetic and copies ran while one was open for 1% -> 9% of each run, Pallas kernels for 0% -> 0%
where the time goes in v1:
time: 131 us
  waiting for transfers between devices  48.8 us (37%)
  blocking collectives  20.4 us (16%)
  matrix products  19.3 us (15%)
  local copies, waits for them, and re-layouts  17.7 us (14%)
  between operations  14.1 us (11%)
  other arithmetic  10.2 us (8%)
    all_gather x1, waiting for transfers between devices, on_device(): rows = lax.all_gather(vectors, ('dp', 'cent'), axis=0, tiled=True)  48.2 us
    all_gather x1, blocking collectives, on_device(): stats = lax.all_gather(jnp.stack([local_peak, local_sum]), 'cent', axis=0)  20.4 us
    unnamed x4, local copies, waits for them, and re-layouts  17.7 us
    dot_general x1, matrix products, on_device(): lax.dot_general(weights, rows, (((1,), (0,)), ((), ())), preferred_elemen...  11.9 us
    dot_general x1, matrix products, on_device(): lax.dot_general(centroids, rows, (((1,), (1,)), ((), ())), preferred_elem...  7.43 us
    convert_element_type x1, other arithmetic, on_device(): return ((own * factor).astype(jnp.bfloat16), loads)  6.29 us
  transfers between devices with their start and end apart: 1, of which 1 were waited for; matrix products, arithmetic and copies ran while one was open for 9% of the time, Pallas kernels for 0%

profile of v1, /device:TPU:0, one launch (start us, length us, event | category | flops | bytes accessed | tf_op | source)
XLA Modules:
  0.0 130.6 jit_solution(8532630208074017856)
XLA Ops:
  7.2 0.0 all-gather.4.cloned.1.call-start
  7.2 0.7 all-gather.4.cloned.1.call-update
  7.9 11.3 %copy.7 = bf16[4096,1024]{0,1:T(8,128)(2,1)} copy(bf16[4096,1024]{1,0:T(8,128)(2,1)} %param.3) | data formatting | bytes 16777216 | tf_op args[1]
  19.2 48.2 %all-gather.4.cloned.1.call-done = bf16[512,1024]{1,0:T(8,128)(2,1)} async-done(((bf16[16,1024]{1,0:T(8,128)(2,1)}), bf16[512,1024]{1,0:T(8,128)(2,1)}) %all-gather.4.cloned.1.call-update) | async-done | bytes 1048592 | tf_op jit(solution)/shard_map/all_gather | solution.py:14
  67.3 7.4 %multiply_reduce_fusion.2 = (f32[512]{0:T(512)S(1)}, f32[4096,512]{1,0:T(8,128)S(1)}) fusion(bf16[4096,1024]{1,0:T(8,128)(2,1)} %param.3, bf16[512,1024]{1,0:T(8,128)(2,1)} %all-gather.4.cloned.1.call-done), kind=kOutput, calls=%fused_computation.6 | convolution fusion | flops 4299161088 | bytes 17827840 | tf_op jit(solution)/shard_map/dot_general | solution.py:16
  74.8 0.0 copy-start
  74.8 1.5 %fusion = f32[512]{0:T(512)S(1)} fusion(f32[4096,512]{1,0:T(8,128)S(1)} %get-tuple-element.10, f32[512]{0:T(512)S(1)} %get-tuple-element.9), kind=kLoop, calls=%fused_computation.7 | loop fusion | flops 6290944 | bytes 8392704 | tf_op jit(solution)/shard_map/reduce_sum | solution.py:23
  76.2 20.4 %all-gather.1 = f32[16,2,512]{2,1,0:T(2,128)S(1)} all-gather(f32[1,2,512]{2,1,0:T(2,128)S(1)} %maximum_bitcast_fusion), channel_id=2, replica_groups=mesh['dp'=2,'cent'=16] {'cent'}, dimensions={0}, use_global_device_ids=true | all-gather | bytes 69632 | tf_op jit(solution)/shard_map/all_gather | solution.py:24
  96.7 0.1 slice_reduce_fusion
  96.8 1.7 %multiply_reduce_fusion.1 = f32[4096]{0:T(1024)S(1)} fusion(f32[4096,512]{1,0:T(8,128)S(1)} %get-tuple-element.10, f32[512]{0:T(512)S(1)} %exponential_divide_fusion, f32[512]{0:T(512)S(1)} %get-tuple-element.9), kind=kLoop, calls=%fused_computation.4 | loop fusion | flops 8384512 | bytes 8409088 | tf_op jit(solution)/shard_map/reduce_sum | solution.py:30
  98.5 0.0 copy-done
  98.5 11.9 %multiply_reduce_fusion = (f32[4096]{0:T(1024)S(1)}, f32[4096,1024]{0,1:T(8,128)}) fusion(bf16[512,1024]{1,0:T(8,128)(2,1)S(1)} %copy-done, f32[4096,512]{1,0:T(8,128)S(1)} %get-tuple-element.10, f32[512]{0:T(512)S(1)} %exponential_divide_fusion, f32[512]{0:T(512)S(1)} %get-tuple-element.9, bf16[4096,1024]{0,1:T(8,128)(2,1)} %copy.7), kind=kOutput, calls=%fused_computation | convolution fusion | flops 4324323328 | bytes 34623488 | tf_op jit(solution)/shard_map/dot_general | solution.py:31
  110.5 6.3 %multiply_convert_fusion = bf16[4096,512]{0,1:T(8,128)(2,1)} fusion(f32[4096,1024]{0,1:T(8,128)} %get-tuple-element.12, s32[]{:T(128)S(6)} %select_n.3, f32[4096]{0:T(1024)S(1)} %add_rsqrt_fusion), kind=kLoop, calls=%fused_computation.2 | loop fusion | flops 4194304 | bytes 12599300 | tf_op jit(solution)/shard_map/convert_element_type | solution.py:38
  116.7 6.4 %copy.9 = bf16[4096,512]{1,0:T(8,128)(2,1)} copy(bf16[4096,512]{0,1:T(8,128)(2,1)} %multiply_convert_fusion) | data formatting | bytes 8388608
  123.1 0.6 broadcast_multiply_fusion
  (4 shorter events, 0.1 us)
Async XLA Ops:
  7.2 60.2 %all-gather.4.cloned.1.call-start = ((), (), s32[]{:S(2)}) async-start(), calls=%async_computation | async-start | bytes 1081344 | tf_op jit(solution)/shard_map/all_gather | solution.py:14
  74.8 23.8 %copy-start = (bf16[512,1024]{1,0:T(8,128)(2,1)S(1)}, bf16[512,1024]{1,0:T(8,128)(2,1)}, u32[]{:S(2)}) copy-start(bf16[512,1024]{1,0:T(8,128)(2,1)} %all-gather.4.cloned.1.call-done) | copy-start | bytes 3145732
Sparse Core Ops, SparseCore 0:
  10.9 56.4 all-gather.3

commit v2 on v1

--- a/solution.py
+++ b/solution.py
@@ -1,12 +1,22 @@
+import functools
+import math
 import jax
 import jax.numpy as jnp
 from jax import lax
+from jax.experimental import pallas as pl
+from jax.experimental.pallas import tpu as pltpu
 from jax.sharding import PartitionSpec as P
 
 softness_scale = 0.1
-
-
-def on_device(vectors, centroids):
+MESH = pl.DeviceIdType.MESH
+LANES = 128
+SCORE_ROWS = 1024
+SUM_ROWS = 512
+EXP_ROWS = 64
+VMEM_BYTES = 56 * 1024 * 1024
+
+
+def plain_form(vectors, centroids):
     dp = lax.axis_size("dp")
     cent = lax.axis_size("cent")
     total_rows = vectors.shape[0] * dp * cent
@@ -38,7 +48,334 @@
     return ((own * factor).astype(jnp.bfloat16), loads)
 
 
+def gather_kernel(
+    cent, nz, vec_hbm, cen_hbm, e_hbm, rows_hbm, resc_ref,
+    cen, scores, expo, rows, stats,
+    local_sem, cen_sem, out_sem, send_sem, recv_sem, sib_send, sib_recv, stat_send, stat_recv,
+):
+    x = lax.axis_index("dp")
+    i = lax.axis_index("cent")
+    c = i % 2
+    y = (i // 2) % 2
+    z = i // 4
+
+    chunks = cen_hbm.shape[0] // SCORE_ROWS
+
+    def cen_copy(j):
+        span = pl.ds(pl.multiple_of(j * SCORE_ROWS, SCORE_ROWS), SCORE_ROWS)
+        return pltpu.make_async_copy(cen_hbm.at[span], cen.at[span], cen_sem.at[j])
+
+    own0 = (z * 2 + y) * 2 + x
+    own1 = (x * 2 + y) * nz + z
+    own = jnp.where(c == 0, own0, own1)
+    mine = pltpu.make_async_copy(vec_hbm, rows.at[c, own], local_sem.at[0])
+    mine.start()
+    for j in range(chunks):
+        cen_copy(j).start()
+
+    barrier = pltpu.get_barrier_semaphore()
+    for o in range(1, cent):
+        pl.semaphore_signal(
+            barrier, inc=1, device_id=(x, lax.rem(i + o, cent)), device_id_type=MESH
+        )
+    pl.semaphore_signal(barrier, inc=1, device_id=(1 - x, i), device_id_type=MESH)
+    mine.wait()
+    pl.semaphore_wait(barrier, cent)
+
+    def at(zz, yy, cc):
+        return (zz * 2 + yy) * 2 + cc
+
+    def send(core, start, count, to, send_at, recv_at):
+        piece = rows.at[core, pl.ds(start, count)]
+        return pltpu.make_async_remote_copy(
+            src_ref=piece, dst_ref=piece, send_sem=send_sem.at[send_at],
+            recv_sem=recv_sem.at[recv_at], device_id=to, device_id_type=MESH,
+        )
+
+    def sibling(core, start, count, slot):
+        piece = rows.at[core, pl.ds(start, count)]
+        return pltpu.make_async_remote_copy(
+            src_ref=piece, dst_ref=piece, send_sem=sib_send.at[slot],
+            recv_sem=sib_recv.at[slot], device_id=(x, at(z, y, 1 - core)), device_id_type=MESH,
+        )
+
+    def along_z(core, first, count, visit):
+        def up(zz):
+            return send(core, first(zz), count, (x, at(z + 1, y, core)), 2 + zz, 2 + zz)
+
+        def down(zz):
+            return send(core, first(zz), count, (x, at(z - 1, y, core)), 2 + nz + zz, 2 + zz)
+
+        for s in range(nz):
+            @pl.when(z - s >= 0)
+            def _():
+                if s:
+                    up(z - s).wait_recv()
+
+                @pl.when(z < nz - 1)
+                def _():
+                    up(z - s).start()
+
+                visit(z - s)
+
+            if s:
+                @pl.when(z + s < nz)
+                def _():
+                    down(z + s).wait_recv()
+
+            @pl.when(jnp.logical_and(z + s < nz, z > 0))
+            def _():
+                down(z + s).start()
+
+            if s:
+                @pl.when(z + s < nz)
+                def _():
+                    visit(z + s)
+
+        def drain():
+            for s in range(nz):
+                @pl.when(jnp.logical_and(z - s >= 0, z < nz - 1))
+                def _():
+                    up(z - s).wait_send()
+
+                @pl.when(jnp.logical_and(z + s < nz, z > 0))
+                def _():
+                    down(z + s).wait_send()
+
+        return drain
+
+    @pl.when(c == 0)
+    def _():
+        over_x = send(0, own0, 1, (1 - x, i), 0, 0)
+        over_x.start()
+        over_x.wait_recv()
+        over_y = send(0, (z * 2 + y) * 2, 2, (x, at(z, 1 - y, 0)), 1, 1)
+        over_y.start()
+        over_y.wait_recv()
+        drain = along_z(
+            0, lambda zz: zz * 4, 4, lambda zz: sibling(0, zz * 4, 4, zz).start()
+        )
+        over_x.wait_send()
+        over_y.wait_send()
+        drain()
+        for zz in range(nz):
+            sibling(0, zz * 4, 4, zz).wait_send()
+        for h in range(2):
+            sibling(1, h * 2 * nz, 2 * nz, h).wait_recv()
+
+    @pl.when(c == 1)
+    def _():
+        drain = along_z(1, lambda zz: (x * 2 + y) * nz + zz, 1, lambda zz: None)
+        over_y = send(1, (x * 2 + y) * nz, nz, (x, at(z, 1 - y, 1)), 1, 1)
+        over_y.start()
+        over_y.wait_recv()
+        over_x = send(1, x * 2 * nz, 2 * nz, (1 - x, i), 0, 0)
+        over_x.start()
+        sibling(1, x * 2 * nz, 2 * nz, x).start()
+        over_x.wait_recv()
+        sibling(1, (1 - x) * 2 * nz, 2 * nz, 1 - x).start()
+        over_x.wait_send()
+        over_y.wait_send()
+        drain()
+        for h in range(2):
+            sibling(1, h * 2 * nz, 2 * nz, h).wait_send()
+        for zz in range(nz):
+            sibling(0, zz * 4, 4, zz).wait_recv()
+
+    total = rows.shape[0] * rows.shape[1] * rows.shape[2]
+    rows_out = pltpu.make_async_copy(rows, rows_hbm, local_sem.at[1])
+    rows_out.start()
+    everything = rows[...].reshape(total, rows.shape[3])
+
+    def score(j, peak):
+        cen_copy(j).wait()
+        span = pl.ds(pl.multiple_of(j * SCORE_ROWS, SCORE_ROWS), SCORE_ROWS)
+        block = lax.dot_general(
+            cen[span], everything, (((1,), (1,)), ((), ())), preferred_element_type=jnp.float32
+        )
+        scores[span] = block
+        return jnp.maximum(peak, jnp.max(block.reshape(-1, 8, total), axis=0))
+
+    peak = lax.fori_loop(0, chunks, score, jnp.full((8, total), -jnp.inf, jnp.float32))
+    peak = jnp.max(peak, axis=0, keepdims=True)
+    scale = math.log2(math.e) / softness_scale
+
+    def e_copy(j):
+        span = pl.ds(pl.multiple_of(j * SCORE_ROWS, SCORE_ROWS), SCORE_ROWS)
+        return pltpu.make_async_copy(expo.at[span], e_hbm.at[span], out_sem.at[j])
+
+    def exponents(j, acc):
+        def part(t, acc):
+            span = pl.ds(pl.multiple_of(j * SCORE_ROWS + t * EXP_ROWS, EXP_ROWS), EXP_ROWS)
+            value = jnp.exp2((scores[span] - peak) * scale)
+            expo[span] = value.astype(jnp.bfloat16)
+            return acc + jnp.sum(value.reshape(-1, 8, total), axis=0)
+
+        acc = lax.fori_loop(0, SCORE_ROWS // EXP_ROWS, part, acc)
+        e_copy(j).start()
+        return acc
+
+    acc = lax.fori_loop(0, chunks, exponents, jnp.zeros((8, total), jnp.float32))
+    acc = jnp.sum(acc, axis=0, keepdims=True)
+
+    groups = total // LANES
+    for g in range(groups):
+        stats[i, g : g + 1, :] = peak[:, g * LANES : (g + 1) * LANES]
+        stats[i, groups + g : groups + g + 1, :] = acc[:, g * LANES : (g + 1) * LANES]
+
+    def stat_copy(o):
+        return pltpu.make_async_remote_copy(
+            src_ref=stats.at[i], dst_ref=stats.at[i], send_sem=stat_send.at[o],
+            recv_sem=stat_recv.at[o], device_id=(x, lax.rem(i + o, cent)), device_id_type=MESH,
+        )
+
+    for o in range(1, cent):
+        stat_copy(o).start()
+    for o in range(1, cent):
+        pltpu.make_async_remote_copy(
+            src_ref=stats.at[i], dst_ref=stats.at[lax.rem(i + cent - o, cent)],
+            send_sem=stat_send.at[o], recv_sem=stat_recv.at[o],
+            device_id=(x, lax.rem(i + o, cent)), device_id_type=MESH,
+        ).wait_recv()
+    peaks = stats[:, 0:groups, :]
+    highest = jnp.max(peaks, axis=0)
+    summed = jnp.sum(stats[:, groups : 2 * groups, :] * jnp.exp2((peaks - highest) * scale), axis=0)
+    resc_ref[...] = jnp.exp2((stats[i, 0:groups, :] - highest) * scale) / summed
+    for o in range(1, cent):
+        stat_copy(o).wait_send()
+    rows_out.wait()
+    for j in range(chunks):
+        e_copy(j).wait()
+
+
+def update_kernel(
+    mass_scale, which, e_ref, resc_ref, cen_own, cen_other, rows_own, rows_other, new_ref, loads_ref
+):
+    j = pl.program_id(0)
+    groups = resc_ref.shape[0]
+    mass = None
+    parts = []
+    for g in range(groups):
+        lanes = slice(g * LANES, (g + 1) * LANES)
+        p = e_ref[:, lanes].astype(jnp.float32) * resc_ref[g : g + 1, :]
+        mass = p if mass is None else mass + p
+        parts.append(p.astype(jnp.bfloat16))
+    weights = jnp.concatenate(parts, axis=1)
+    for b in range(mass.shape[0] // LANES):
+        block = mass[b * LANES : (b + 1) * LANES].T
+        loads_ref[j, b : b + 1, :] = jnp.sum(block, axis=0, keepdims=True) * mass_scale
+    own = cen_own[...].astype(jnp.float32) + mass_scale * jnp.dot(
+        weights, rows_own[...], preferred_element_type=jnp.float32
+    )
+    other = cen_other[...].astype(jnp.float32) + mass_scale * jnp.dot(
+        weights, rows_other[...], preferred_element_type=jnp.float32
+    )
+    width = own.shape[1] + other.shape[1]
+    square = (
+        jnp.sum(own * own, axis=1, keepdims=True) + jnp.sum(other * other, axis=1, keepdims=True)
+    ) / width
+    new_ref[...] = (own * lax.rsqrt(square + 1e-06)).astype(new_ref.dtype)
+
+
+def kernel_form(vectors, centroids):
+    dp = lax.axis_size("dp")
+    cent = lax.axis_size("cent")
+    nz = cent // 4
+    block_rows, width = vectors.shape
+    total = block_rows * dp * cent
+    local = centroids.shape[0]
+    mass_scale = local * cent / total
+    chunks = local // SCORE_ROWS
+    groups = total // LANES
+    e, rows, resc = pl.pallas_call(
+        functools.partial(gather_kernel, cent, nz),
+        out_shape=(
+            jax.ShapeDtypeStruct((local, total), jnp.bfloat16),
+            jax.ShapeDtypeStruct((2, 4 * nz, block_rows, width), jnp.bfloat16),
+            jax.ShapeDtypeStruct((groups, LANES), jnp.float32),
+        ),
+        in_specs=[pl.BlockSpec(memory_space=pl.ANY)] * 2,
+        out_specs=(
+            pl.BlockSpec(memory_space=pl.ANY),
+            pl.BlockSpec(memory_space=pl.ANY),
+            pl.BlockSpec(memory_space=pltpu.VMEM),
+        ),
+        scratch_shapes=[
+            pltpu.VMEM((local, width), jnp.bfloat16),
+            pltpu.VMEM((local, total), jnp.float32),
+            pltpu.VMEM((local, total), jnp.bfloat16),
+            pltpu.VMEM((2, 4 * nz, block_rows, width), jnp.bfloat16),
+            pltpu.VMEM((cent, 2 * groups, LANES), jnp.float32),
+            pltpu.SemaphoreType.DMA((2,)),
+            pltpu.SemaphoreType.DMA((chunks,)),
+            pltpu.SemaphoreType.DMA((chunks,)),
+            pltpu.SemaphoreType.DMA((2 + 2 * nz,)),
+            pltpu.SemaphoreType.DMA((2 + nz,)),
+            pltpu.SemaphoreType.DMA((nz,)),
+            pltpu.SemaphoreType.DMA((nz,)),
+            pltpu.SemaphoreType.DMA((cent,)),
+            pltpu.SemaphoreType.DMA((cent,)),
+        ],
+        compiler_params=pltpu.CompilerParams(
+            collective_id=0, has_side_effects=True, vmem_limit_bytes=VMEM_BYTES
+        ),
+        cost_estimate=pl.CostEstimate(
+            flops=2 * local * total * width, bytes_accessed=2 * local * (width + total),
+            transcendentals=local * total,
+        ),
+    )(vectors, centroids)
+    rows = rows.reshape(total, width)
+    half = width // 2
+    steps = local // SUM_ROWS
+    which = jnp.reshape(lax.axis_index("dp"), (1,)).astype(jnp.int32)
+    new, loads = pl.pallas_call(
+        functools.partial(update_kernel, mass_scale),
+        out_shape=(
+            jax.ShapeDtypeStruct((local, half), jnp.bfloat16),
+            jax.ShapeDtypeStruct((steps, SUM_ROWS // LANES, LANES), jnp.float32),
+        ),
+        grid_spec=pltpu.PrefetchScalarGridSpec(
+            num_scalar_prefetch=1,
+            grid=(steps,),
+            in_specs=[
+                pl.BlockSpec((SUM_ROWS, total), lambda j, d: (j, 0)),
+                pl.BlockSpec((groups, LANES), lambda j, d: (0, 0)),
+                pl.BlockSpec((SUM_ROWS, half), lambda j, d: (j, d[0])),
+                pl.BlockSpec((SUM_ROWS, half), lambda j, d: (j, 1 - d[0])),
+                pl.BlockSpec((total, half), lambda j, d: (0, d[0])),
+                pl.BlockSpec((total, half), lambda j, d: (0, 1 - d[0])),
+            ],
+            out_specs=(
+                pl.BlockSpec((SUM_ROWS, half), lambda j, d: (j, 0)),
+                pl.BlockSpec((steps, SUM_ROWS // LANES, LANES), lambda j, d: (0, 0, 0)),
+            ),
+        ),
+        compiler_params=pltpu.CompilerParams(vmem_limit_bytes=VMEM_BYTES),
+        cost_estimate=pl.CostEstimate(
+            flops=2 * local * total * width, bytes_accessed=2 * local * (width + total + half),
+            transcendentals=local,
+        ),
+    )(which, e, resc, centroids, centroids, rows, rows)
+    return (new, loads.reshape(local))
+
+
 def solution(mesh):
+    dp, cent = mesh.shape["dp"], mesh.shape["cent"]
+
+    def on_device(vectors, centroids):
+        total = vectors.shape[0] * dp * cent
+        fits = (
+            dp == 2
+            and cent % 4 == 0
+            and cent >= 8
+            and vectors.shape[0] % 16 == 0
+            and total % LANES == 0
+            and total <= 1024
+            and centroids.shape[0] % SCORE_ROWS == 0
+            and centroids.shape[0] <= 4096
+        )
+        return (kernel_form if fits else plain_form)(vectors, centroids)
+
     placed = (P(("dp", "cent"), None), P("cent", None))
     return jax.shard_map(
         on_device,

time: 131 us -> 51.2 us (0.39)
  Pallas kernels: 0 us -> 50.3 us
  waiting for transfers between devices: 48.8 us -> 0 us
  blocking collectives: 20.4 us -> 0 us
  matrix products: 19.3 us -> 0 us
  local copies, waits for them, and re-layouts: 17.7 us -> 0 us
  between operations: 14.1 us -> 0.64 us
  other arithmetic: 10.2 us -> 0 us
    pallas_call x0 -> x2, Pallas kernels: none -> 50.3 us  [the longest x1 38 us: kernel_form(): pl.pallas_call(functools.partial(gather_kernel, cent, nz), out_shape=(jax...]
    all_gather x1 -> x0, waiting for transfers between devices: 48.2 us -> none  [on_device(): rows = lax.all_gather(vectors, ('dp', 'cent'), axis=0, tiled=True)]
    all_gather x1 -> x0, blocking collectives: 20.4 us -> none  [on_device(): stats = lax.all_gather(jnp.stack([local_peak, local_sum]), 'cent', axis=0)]
    dot_general x2 -> x0, matrix products: 19.3 us -> none  [the longest x1 11.9 us: on_device(): lax.dot_general(weights, rows, (((1,), (0,)), ((), ())), preferred_elemen...]
    unnamed x4 -> x0, local copies, waits for them, and re-layouts: 17.7 us -> none
    convert_element_type x1 -> x0, other arithmetic: 6.29 us -> none  [on_device(): return ((own * factor).astype(jnp.bfloat16), loads)]
    reduce_sum x3 -> x0, other arithmetic: 3.2 us -> none  [the longest x1 1.72 us: on_device(): loads = jnp.sum(probability, axis=1) * mass_scale]
  transfers between devices with their start and end apart: 1 -> 0, of which waited for: 1 -> 0; matrix products, arithmetic and copies ran while one was open for 9% -> 0% of each run, Pallas kernels for 0% -> 0%
where the time goes in v2:
time: 51.2 us; the launch traced here: 50.9 us
  Pallas kernels  50.3 us (98%)
  between operations  0.64 us (1%)
    pallas_call x1, Pallas kernels, kernel_form(): pl.pallas_call(functools.partial(gather_kernel, cent, nz), out_shape=(jax...  38 us
    pallas_call x1, Pallas kernels, kernel_form(): pl.pallas_call(functools.partial(update_kernel, mass_scale), out_shape=(j...  12.2 us

profile of v2, /device:TPU:0, one launch (start us, length us, event | category | flops | bytes accessed | tf_op | source)
XLA Modules:
  0.0 50.9 jit_solution(18186191068241060363)
XLA Ops:
  0.6 38.0 %shard_map.41 = (bf16[4096,512]{1,0:T(8,128)(2,1)}, bf16[2,16,16,1024]{3,2,1,0:T(8,128)(2,1)}, f32[4,128]{1,0:T(4,128)}) custom-call(bf16[16,1024]{1,0:T(8,128)(2,1)} %vec_hbm.1, bf16[4096,1024]{1,0:T(8,128)(2,1)} %cen_other.1), custom_call_target="tpu_custom_call" | custom-call | flops 4294967296 | bytes 12582912 | tf_op jit(solution)/shard_map/pallas_call | solution.py:290
  38.6 12.2 %shard_map.42 = (bf16[4096,512]{1,0:T(8,128)(2,1)}, f32[8,4,128]{2,1,0:T(4,128)}) custom-call(s32[1]{0:T(128)} %bitcast.which, bf16[4096,512]{1,0:T(8,128)(2,1)} %get-tuple-element.7.e_ref, f32[4,128]{1,0:T(4,128)} %get-tuple-element.8.resc_ref, bf16[4096,1024]{1,0:T(8,128)(2,1)} %cen_other.1, bf16[4096,1024]{1,0:T(8,128)(2,1)} %cen_other.1, ...), custom_call_target="tpu_custom_call" | custom-call | flops 4294967296 | bytes 16777216 | tf_op jit(solution)/shard_map/pallas_call | solution.py:331

commit v3 on v2

v3 whole, which is shorter than its diff:
```python
import functools
import math
import jax
import jax.numpy as jnp
from jax import lax
from jax.experimental import pallas as pl
from jax.experimental.pallas import tpu as pltpu
from jax.sharding import PartitionSpec as P

softness_scale = 0.1
MESH = pl.DeviceIdType.MESH
LANES = 128
SCORE_ROWS = 1024
SUM_ROWS = 1024
EXP_ROWS = 64
VMEM_BYTES = 56 * 1024 * 1024


def plain_form(vectors, centroids):
    dp = lax.axis_size("dp")
    cent = lax.axis_size("cent")
    total_rows = vectors.shape[0] * dp * cent
    mass_scale = centroids.shape[0] * cent / total_rows
    rows = lax.all_gather(vectors, ("dp", "cent"), axis=0, tiled=True)
    scores = (
        lax.dot_general(
            centroids, rows, (((1,), (1,)), ((), ())), preferred_element_type=jnp.float32
        )
        / softness_scale
    )
    local_peak = jnp.max(scores, axis=0)
    exponent = jnp.exp(scores - local_peak[None, :])
    local_sum = jnp.sum(exponent, axis=0)
    stats = lax.all_gather(jnp.stack([local_peak, local_sum]), "cent", axis=0)
    highest = jnp.max(stats[:, 0], axis=0)
    summed = jnp.sum(stats[:, 1] * jnp.exp(stats[:, 0] - highest[None, :]), axis=0)
    rescale = jnp.exp(local_peak - highest) / summed
    probability = exponent * rescale[None, :]
    weights = probability.astype(jnp.bfloat16)
    loads = jnp.sum(probability, axis=1) * mass_scale
    sums = lax.dot_general(
        weights, rows, (((1,), (0,)), ((), ())), preferred_element_type=jnp.float32
    )
    shifted = centroids.astype(jnp.float32) + sums * mass_scale
    factor = lax.rsqrt(jnp.mean(shifted * shifted, axis=1, keepdims=True) + 1e-06)
    columns = centroids.shape[1] // dp
    own = lax.dynamic_slice_in_dim(shifted, lax.axis_index("dp") * columns, columns, 1)
    return ((own * factor).astype(jnp.bfloat16), loads)


def gather_kernel(
    cent, nz, mass_scale, vec_hbm, cen_hbm, e_hbm, rows_hbm, resc_ref,
    cen, scores, expo, rows, stats, resc,
    local_sem, cen_sem, out_sem, z_send, z_recv, xy_send, xy_recv, relay_send, relay_recv,
    sib_send, sib_recv, stat_send, stat_recv,
):
    x = lax.axis_index("dp")
    i = lax.axis_index("cent")
    c = i % 2
    y = (i // 2) % 2
    z = i // 4
    total = scores.shape[1]
    pair = 2 * LANES
    chunks = cen_hbm.shape[0] // SCORE_ROWS

    def chunk_span(j):
        return pl.ds(pl.multiple_of(j * SCORE_ROWS, SCORE_ROWS), SCORE_ROWS)

    def cen_copy(j):
        return pltpu.make_async_copy(
            cen_hbm.at[chunk_span(j)], cen.at[chunk_span(j)], cen_sem.at[j]
        )

    own = x * 2 + y
    mine = pltpu.make_async_copy(vec_hbm, rows.at[z, c, own], local_sem.at[0])
    mine.start()
    for j in range(chunks):
        cen_copy(j).start()

    barrier = pltpu.get_barrier_semaphore()
    for o in range(1, cent):
        pl.semaphore_signal(
            barrier, inc=1, device_id=(x, lax.rem(i + o, cent)), device_id_type=MESH
        )
    pl.semaphore_signal(barrier, inc=1, device_id=(1 - x, i), device_id_type=MESH)
    mine.wait()
    pl.semaphore_wait(barrier, cent)

    def slab(o):
        return lax.rem(z + nz - o, nz)

    def remote(piece, send_sem, recv_sem, to):
        return pltpu.make_async_remote_copy(
            src_ref=piece, dst_ref=piece, send_sem=send_sem, recv_sem=recv_sem,
            device_id=to, device_id_type=MESH,
        )

    x_peer = (1 - x, i)
    y_peer = (x, (z * 2 + 1 - y) * 2 + c)

    def over_z(o):
        to = (x, (lax.rem(z + o, nz) * 2 + y) * 2 + c)
        return remote(rows.at[z, c, own], z_send.at[o], z_recv.at[o], to)

    def over_x(o):
        return remote(rows.at[slab(o), c, own], xy_send.at[0, o], xy_recv.at[0, o], x_peer)

    def over_y(o):
        return remote(rows.at[slab(o), c, own], xy_send.at[1, o], xy_recv.at[1, o], y_peer)

    def arrived(way, o):
        source = jnp.where(way == 0, (1 - x) * 2 + y, x * 2 + 1 - y)
        piece = rows.at[slab(o), c, source]
        return remote(piece, xy_send.at[way, o], xy_recv.at[way, o], x_peer)

    relay_source = jnp.where(c == 0, (1 - x) * 2 + y, x * 2 + 1 - y)
    relay_to = (jnp.where(c == 0, x, 1 - x), jnp.where(c == 0, y_peer[1], i))

    def relay(o):
        return remote(
            rows.at[slab(o), c, relay_source], relay_send.at[o], relay_recv.at[o], relay_to
        )

    def relayed(o):
        piece = rows.at[slab(o), c, (1 - x) * 2 + 1 - y]
        return remote(piece, relay_send.at[o], relay_recv.at[o], relay_to)

    def sibling(o, core):
        to = (x, i + 1 - 2 * c)
        return remote(rows.at[slab(o), core], sib_send.at[o], sib_recv.at[o], to)

    def z_arrival(o):
        piece = rows.at[slab(o), c, own]
        return remote(piece, z_send.at[o], z_recv.at[o], y_peer)

    def forward(o):
        if o:
            z_arrival(o).wait_recv()
        over_x(o).start()
        over_y(o).start()

    def pass_on(o):
        arrived(c, o).wait_recv()
        relay(o).start()

    def complete(o):
        arrived(1 - c, o).wait_recv()
        relayed(o).wait_recv()
        sibling(o, c).start()

    def rows_copy(o):
        return pltpu.make_async_copy(rows.at[slab(o)], rows_hbm.at[o], local_sem.at[1 + o])

    def usable(o):
        sibling(o, 1 - c).wait_recv()
        rows_copy(o).start()

    forward(0)
    for o in range(1, nz):
        over_z(o).start()
    for o in range(1, nz):
        forward(o)
        pass_on(o - 1)
    complete(0)
    complete(1)

    def score(p, j, peak):
        if p == 0:
            cen_copy(j).wait()
        two = [rows[slab(2 * p + t)].reshape(LANES, rows.shape[4]) for t in range(2)]
        block = lax.dot_general(
            cen[chunk_span(j)], jnp.concatenate(two, axis=0), (((1,), (1,)), ((), ())),
            preferred_element_type=jnp.float32,
        )
        scores[chunk_span(j), p * pair : (p + 1) * pair] = block
        return jnp.maximum(peak, jnp.max(block.reshape(-1, 8, pair), axis=0))

    scale = math.log2(math.e) / softness_scale

    def e_copy(j):
        return pltpu.make_async_copy(
            expo.at[chunk_span(j)], e_hbm.at[chunk_span(j)], out_sem.at[j]
        )

    def exponents(p, peak, last):
        columns = slice(p * pair, (p + 1) * pair)

        def whole(j, acc):
            def part(t, acc):
                span = pl.ds(pl.multiple_of(j * SCORE_ROWS + t * EXP_ROWS, EXP_ROWS), EXP_ROWS)
                value = jnp.exp2((scores[span, columns] - peak) * scale)
                expo[span, columns] = value.astype(jnp.bfloat16)
                return acc + jnp.sum(value.reshape(-1, 8, pair), axis=0)

            acc = lax.fori_loop(0, SCORE_ROWS // EXP_ROWS, part, acc)
            if last:
                e_copy(j).start()
            return acc

        acc = lax.fori_loop(0, chunks, whole, jnp.zeros((8, pair), jnp.float32))
        acc = jnp.sum(acc, axis=0, keepdims=True)
        for t in range(2):
            lanes = slice(t * LANES, (t + 1) * LANES)
            at = slab(2 * p + t)
            stats[i, pl.ds(at, 1), :] = peak[:, lanes]
            stats[i, pl.ds(nz + at, 1), :] = acc[:, lanes]

    later = [functools.partial(pass_on, nz - 1)]
    later += [functools.partial(complete, o) for o in range(2, nz)]
    for p in range(nz // 2):
        for t in range(2):
            usable(2 * p + t)
        peak = jnp.full((8, pair), -jnp.inf, jnp.float32)
        for j in range(chunks):
            peak = score(p, j, peak)
            if later:
                later.pop(0)()
        while later:
            later.pop(0)()
        peak = jnp.max(peak, axis=0, keepdims=True)
        exponents(p, peak, p == nz // 2 - 1)

    def stat_copy(o, slot):
        return pltpu.make_async_remote_copy(
            src_ref=stats.at[i], dst_ref=stats.at[slot], send_sem=stat_send.at[o],
            recv_sem=stat_recv.at[o], device_id=(x, lax.rem(i + o, cent)), device_id_type=MESH,
        )

    for o in range(1, cent):
        stat_copy(o, i).start()
    for o in range(1, cent):
        stat_copy(o, lax.rem(i + cent - o, cent)).wait_recv()
    peaks = stats[:, 0:nz, :]
    highest = jnp.max(peaks, axis=0)
    summed = jnp.sum(stats[:, nz : 2 * nz, :] * jnp.exp2((peaks - highest) * scale), axis=0)
    resc[...] = jnp.exp2((stats[i, 0:nz, :] - highest) * scale) * (mass_scale / summed)
    for o in range(nz):
        resc_ref[o : o + 1, :] = resc[pl.ds(slab(o), 1), :]
    for o in range(1, cent):
        stat_copy(o, i).wait_send()
    for o in range(nz):
        if o:
            over_z(o).wait_send()
        over_x(o).wait_send()
        over_y(o).wait_send()
        relay(o).wait_send()
        sibling(o, c).wait_send()
        rows_copy(o).wait()
    for j in range(chunks):
        e_copy(j).wait()


def update_kernel(
    which, e_ref, resc_ref, cen_own, cen_other, rows_own, rows_other, new_ref, loads_ref
):
    j = pl.program_id(0)
    groups = resc_ref.shape[0]
    mass = None
    parts = []
    for g in range(groups):
        lanes = slice(g * LANES, (g + 1) * LANES)
        p = e_ref[:, lanes].astype(jnp.float32) * resc_ref[g : g + 1, :]
        mass = p if mass is None else mass + p
        parts.append(p.astype(jnp.bfloat16))
    weights = jnp.concatenate(parts, axis=1)
    for b in range(mass.shape[0] // LANES):
        block = mass[b * LANES : (b + 1) * LANES].T
        loads_ref[j, b : b + 1, :] = jnp.sum(block, axis=0, keepdims=True)
    own = cen_own[...].astype(jnp.float32) + jnp.dot(
        weights, rows_own[...], preferred_element_type=jnp.float32
    )
    other = cen_other[...].astype(jnp.float32) + jnp.dot(
        weights, rows_other[...], preferred_element_type=jnp.float32
    )
    width = own.shape[1] + other.shape[1]
    square = (
        jnp.sum(own * own, axis=1, keepdims=True) + jnp.sum(other * other, axis=1, keepdims=True)
    ) / width
    new_ref[...] = (own * lax.rsqrt(square + 1e-06)).astype(new_ref.dtype)


def kernel_form(vectors, centroids):
    dp = lax.axis_size("dp")
    cent = lax.axis_size("cent")
    nz = cent // 4
    block_rows, width = vectors.shape
    total = block_rows * dp * cent
    local = centroids.shape[0]
    mass_scale = local * cent / total
    chunks = local // SCORE_ROWS
    groups = total // LANES
    e, rows, resc = pl.pallas_call(
        functools.partial(gather_kernel, cent, nz, mass_scale),
        out_shape=(
            jax.ShapeDtypeStruct((local, total), jnp.bfloat16),
            jax.ShapeDtypeStruct((nz, 2, 4, block_rows, width), jnp.bfloat16),
            jax.ShapeDtypeStruct((groups, LANES), jnp.float32),
        ),
        in_specs=[pl.BlockSpec(memory_space=pl.ANY)] * 2,
        out_specs=(
            pl.BlockSpec(memory_space=pl.ANY),
            pl.BlockSpec(memory_space=pl.ANY),
            pl.BlockSpec(memory_space=pltpu.VMEM),
        ),
        scratch_shapes=[
            pltpu.VMEM((local, width), jnp.bfloat16),
            pltpu.VMEM((local, total), jnp.float32),
            pltpu.VMEM((local, total), jnp.bfloat16),
            pltpu.VMEM((nz, 2, 4, block_rows, width), jnp.bfloat16),
            pltpu.VMEM((cent, 2 * groups, LANES), jnp.float32),
            pltpu.VMEM((groups, LANES), jnp.float32),
            pltpu.SemaphoreType.DMA((1 + nz,)),
            pltpu.SemaphoreType.DMA((chunks,)),
            pltpu.SemaphoreType.DMA((chunks,)),
            pltpu.SemaphoreType.DMA((nz,)),
            pltpu.SemaphoreType.DMA((nz,)),
            pltpu.SemaphoreType.DMA((2, nz)),
            pltpu.SemaphoreType.DMA((2, nz)),
            pltpu.SemaphoreType.DMA((nz,)),
            pltpu.SemaphoreType.DMA((nz,)),
            pltpu.SemaphoreType.DMA((nz,)),
            pltpu.SemaphoreType.DMA((nz,)),
            pltpu.SemaphoreType.DMA((cent,)),
            pltpu.SemaphoreType.DMA((cent,)),
        ],
        compiler_params=pltpu.CompilerParams(
            collective_id=0, has_side_effects=True, vmem_limit_bytes=VMEM_BYTES
        ),
        cost_estimate=pl.CostEstimate(
            flops=2 * local * total * width, bytes_accessed=2 * local * (width + total),
            transcendentals=local * total,
        ),
    )(vectors, centroids)
    rows = rows.reshape(total, width)
    half = width // 2
    steps = local // SUM_ROWS
    which = jnp.reshape(lax.axis_index("dp"), (1,)).astype(jnp.int32)
    new, loads = pl.pallas_call(
        update_kernel,
        out_shape=(
            jax.ShapeDtypeStruct((local, half), jnp.bfloat16),
            jax.ShapeDtypeStruct((steps, SUM_ROWS // LANES, LANES), jnp.float32),
        ),
        grid_spec=pltpu.PrefetchScalarGridSpec(
            num_scalar_prefetch=1,
            grid=(steps,),
            in_specs=[
                pl.BlockSpec((SUM_ROWS, total), lambda j, d: (j, 0)),
                pl.BlockSpec((groups, LANES), lambda j, d: (0, 0)),
                pl.BlockSpec((SUM_ROWS, half), lambda j, d: (j, d[0])),
                pl.BlockSpec((SUM_ROWS, half), lambda j, d: (j, 1 - d[0])),
                pl.BlockSpec((total, half), lambda j, d: (0, d[0])),
                pl.BlockSpec((total, half), lambda j, d: (0, 1 - d[0])),
            ],
            out_specs=(
                pl.BlockSpec((SUM_ROWS, half), lambda j, d: (j, 0)),
                pl.BlockSpec((steps, SUM_ROWS // LANES, LANES), lambda j, d: (0, 0, 0)),
            ),
        ),
        compiler_params=pltpu.CompilerParams(vmem_limit_bytes=VMEM_BYTES),
        cost_estimate=pl.CostEstimate(
            flops=2 * local * total * width, bytes_accessed=2 * local * (width + total + half),
            transcendentals=local,
        ),
    )(which, e, resc, centroids, centroids, rows, rows)
    return (new, loads.reshape(local))


def solution(mesh):
    dp, cent = mesh.shape["dp"], mesh.shape["cent"]

    def on_device(vectors, centroids):
        total = vectors.shape[0] * dp * cent
        fits = (
            dp == 2
            and cent % 8 == 0
            and vectors.shape[0] * 8 == LANES
            and total <= 1024
            and centroids.shape[0] % SCORE_ROWS == 0
            and centroids.shape[0] <= 4096
        )
        return (kernel_form if fits else plain_form)(vectors, centroids)

    placed = (P(("dp", "cent"), None), P("cent", None))
    return jax.shard_map(
        on_device,
        mesh=mesh,
        in_specs=placed,
        out_specs=(P("cent", "dp"), P("cent")),
        check_vma=False,
    )
```

time: 51.2 us -> 42.9 us (0.84)
  Pallas kernels: 50.3 us -> 42.1 us
    pallas_call x2, Pallas kernels: 50.3 us -> 42.1 us  [the longest x1 31.7 us: kernel_form(): pl.pallas_call(functools.partial(gather_kernel, cent, nz, mass_scale), ou...]
where the time goes in v3:
time: 42.9 us; the launch traced here: 42.7 us
  Pallas kernels  42.1 us (98%)
  between operations  0.64 us (1%)
    pallas_call x1, Pallas kernels, kernel_form(): pl.pallas_call(functools.partial(gather_kernel, cent, nz, mass_scale), ou...  31.7 us
    pallas_call x1, Pallas kernels, kernel_form(): pl.pallas_call(update_kernel, out_shape=(jax.ShapeDtypeStruct((local, hal...  10.4 us

profile of v3, /device:TPU:0, one launch (start us, length us, event | category | flops | bytes accessed | tf_op | source)
XLA Modules:
  0.0 42.7 jit_solution(15042787636429343750)
XLA Ops:
  0.6 31.7 %shard_map.41 = (bf16[4096,512]{1,0:T(8,128)(2,1)}, bf16[4,2,4,16,1024]{4,3,2,1,0:T(8,128)(2,1)}, f32[4,128]{1,0:T(4,128)}) custom-call(bf16[16,1024]{1,0:T(8,128)(2,1)} %vec_hbm.1, bf16[4096,1024]{1,0:T(8,128)(2,1)} %cen_other.1), custom_call_target="tpu_custom_call" | custom-call | flops 4294967296 | bytes 12582912 | tf_op jit(solution)/shard_map/pallas_call | solution.py:292
  32.3 10.4 %shard_map.42 = (bf16[4096,512]{1,0:T(8,128)(2,1)}, f32[4,8,128]{2,1,0:T(8,128)}) custom-call(s32[1]{0:T(128)} %bitcast.which, bf16[4096,512]{1,0:T(8,128)(2,1)} %get-tuple-element.7.e_ref, f32[4,128]{1,0:T(4,128)} %get-tuple-element.8.resc_ref, bf16[4096,1024]{1,0:T(8,128)(2,1)} %cen_other.1, bf16[4096,1024]{1,0:T(8,128)(2,1)} %cen_other.1, ...), custom_call_target="tpu_custom_call" | custom-call | flops 4294967296 | bytes 16777216 | tf_op jit(solution)/shard_map/pallas_call | solution.py:338

commit v4 on v3

--- a/solution.py
+++ b/solution.py
@@ -60,7 +60,8 @@
     y = (i // 2) % 2
     z = i // 4
     total = scores.shape[1]
-    pair = 2 * LANES
+    pair = total // 2
+    per = pair // LANES
     chunks = cen_hbm.shape[0] // SCORE_ROWS
 
     def chunk_span(j):
@@ -72,7 +73,7 @@
         )
 
     own = x * 2 + y
-    mine = pltpu.make_async_copy(vec_hbm, rows.at[z, c, own], local_sem.at[0])
+    mine = pltpu.make_async_copy(vec_hbm, rows.at[c, z, own], local_sem.at[0])
     mine.start()
     for j in range(chunks):
         cen_copy(j).start()
@@ -87,7 +88,7 @@
     pl.semaphore_wait(barrier, cent)
 
     def slab(o):
-        return lax.rem(z + nz - o, nz)
+        return lax.rem(jnp.where(z < nz // 2, z + o, z + nz - o), nz)
 
     def remote(piece, send_sem, recv_sem, to):
         return pltpu.make_async_remote_copy(
@@ -99,18 +100,18 @@
     y_peer = (x, (z * 2 + 1 - y) * 2 + c)
 
     def over_z(o):
-        to = (x, (lax.rem(z + o, nz) * 2 + y) * 2 + c)
-        return remote(rows.at[z, c, own], z_send.at[o], z_recv.at[o], to)
+        to = (x, (slab(o) * 2 + y) * 2 + c)
+        return remote(rows.at[c, z, own], z_send.at[o], z_recv.at[z], to)
 
     def over_x(o):
-        return remote(rows.at[slab(o), c, own], xy_send.at[0, o], xy_recv.at[0, o], x_peer)
+        return remote(rows.at[c, slab(o), own], xy_send.at[0, o], xy_recv.at[0, o], x_peer)
 
     def over_y(o):
-        return remote(rows.at[slab(o), c, own], xy_send.at[1, o], xy_recv.at[1, o], y_peer)
+        return remote(rows.at[c, slab(o), own], xy_send.at[1, o], xy_recv.at[1, o], y_peer)
 
     def arrived(way, o):
         source = jnp.where(way == 0, (1 - x) * 2 + y, x * 2 + 1 - y)
-        piece = rows.at[slab(o), c, source]
+        piece = rows.at[c, slab(o), source]
         return remote(piece, xy_send.at[way, o], xy_recv.at[way, o], x_peer)
 
     relay_source = jnp.where(c == 0, (1 - x) * 2 + y, x * 2 + 1 - y)
@@ -118,20 +119,20 @@
 
     def relay(o):
         return remote(
-            rows.at[slab(o), c, relay_source], relay_send.at[o], relay_recv.at[o], relay_to
+            rows.at[c, slab(o), relay_source], relay_send.at[o], relay_recv.at[o], relay_to
         )
 
     def relayed(o):
-        piece = rows.at[slab(o), c, (1 - x) * 2 + 1 - y]
+        piece = rows.at[c, slab(o), (1 - x) * 2 + 1 - y]
         return remote(piece, relay_send.at[o], relay_recv.at[o], relay_to)
 
     def sibling(o, core):
         to = (x, i + 1 - 2 * c)
-        return remote(rows.at[slab(o), core], sib_send.at[o], sib_recv.at[o], to)
+        return remote(rows.at[core, slab(o)], sib_send.at[o], sib_recv.at[o], to)
 
     def z_arrival(o):
-        piece = rows.at[slab(o), c, own]
-        return remote(piece, z_send.at[o], z_recv.at[o], y_peer)
+        piece = rows.at[c, slab(o), own]
+        return remote(piece, z_send.at[o], z_recv.at[slab(o)], y_peer)
 
     def forward(o):
         if o:
@@ -148,12 +149,11 @@
         relayed(o).wait_recv()
         sibling(o, c).start()
 
-    def rows_copy(o):
-        return pltpu.make_async_copy(rows.at[slab(o)], rows_hbm.at[o], local_sem.at[1 + o])
-
-    def usable(o):
-        sibling(o, 1 - c).wait_recv()
-        rows_copy(o).start()
+    def core_of(p):
+        return c if p == 0 else 1 - c
+
+    def rows_copy(p):
+        return pltpu.make_async_copy(rows.at[core_of(p)], rows_hbm.at[p], local_sem.at[1 + p])
 
     forward(0)
     for o in range(1, nz):
@@ -161,15 +161,15 @@
     for o in range(1, nz):
         forward(o)
         pass_on(o - 1)
-    complete(0)
-    complete(1)
+    pass_on(nz - 1)
+    for o in range(nz):
+        complete(o)
 
     def score(p, j, peak):
         if p == 0:
             cen_copy(j).wait()
-        two = [rows[slab(2 * p + t)].reshape(LANES, rows.shape[4]) for t in range(2)]
         block = lax.dot_general(
-            cen[chunk_span(j)], jnp.concatenate(two, axis=0), (((1,), (1,)), ((), ())),
+            cen[chunk_span(j)], rows[core_of(p)].reshape(pair, rows.shape[4]), (((1,), (1,)), ((), ())),
             preferred_element_type=jnp.float32,
         )
         scores[chunk_span(j), p * pair : (p + 1) * pair] = block
@@ -199,26 +199,22 @@
 
         acc = lax.fori_loop(0, chunks, whole, jnp.zeros((8, pair), jnp.float32))
         acc = jnp.sum(acc, axis=0, keepdims=True)
-        for t in range(2):
+        for t in range(per):
             lanes = slice(t * LANES, (t + 1) * LANES)
-            at = slab(2 * p + t)
+            at = core_of(p) * per + t
             stats[i, pl.ds(at, 1), :] = peak[:, lanes]
-            stats[i, pl.ds(nz + at, 1), :] = acc[:, lanes]
-
-    later = [functools.partial(pass_on, nz - 1)]
-    later += [functools.partial(complete, o) for o in range(2, nz)]
-    for p in range(nz // 2):
-        for t in range(2):
-            usable(2 * p + t)
+            stats[i, pl.ds(2 * per + at, 1), :] = acc[:, lanes]
+
+    for p in range(2):
+        if p:
+            for o in range(nz):
+                sibling(o, 1 - c).wait_recv()
+        rows_copy(p).start()
         peak = jnp.full((8, pair), -jnp.inf, jnp.float32)
         for j in range(chunks):
             peak = score(p, j, peak)
-            if later:
-                later.pop(0)()
-        while later:
-            later.pop(0)()
         peak = jnp.max(peak, axis=0, keepdims=True)
-        exponents(p, peak, p == nz // 2 - 1)
+        exponents(p, peak, p == 1)
 
     def stat_copy(o, slot):
         return pltpu.make_async_remote_copy(
@@ -230,12 +226,14 @@
         stat_copy(o, i).start()
     for o in range(1, cent):
         stat_copy(o, lax.rem(i + cent - o, cent)).wait_recv()
-    peaks = stats[:, 0:nz, :]
+    peaks = stats[:, 0 : 2 * per, :]
     highest = jnp.max(peaks, axis=0)
-    summed = jnp.sum(stats[:, nz : 2 * nz, :] * jnp.exp2((peaks - highest) * scale), axis=0)
-    resc[...] = jnp.exp2((stats[i, 0:nz, :] - highest) * scale) * (mass_scale / summed)
-    for o in range(nz):
-        resc_ref[o : o + 1, :] = resc[pl.ds(slab(o), 1), :]
+    summed = jnp.sum(stats[:, 2 * per : 4 * per, :] * jnp.exp2((peaks - highest) * scale), axis=0)
+    resc[...] = jnp.exp2((stats[i, 0 : 2 * per, :] - highest) * scale) * (mass_scale / summed)
+    for p in range(2):
+        for t in range(per):
+            g = p * per + t
+            resc_ref[g : g + 1, :] = resc[pl.ds(core_of(p) * per + t, 1), :]
     for o in range(1, cent):
         stat_copy(o, i).wait_send()
     for o in range(nz):
@@ -245,7 +243,8 @@
         over_y(o).wait_send()
         relay(o).wait_send()
         sibling(o, c).wait_send()
-        rows_copy(o).wait()
+    for p in range(2):
+        rows_copy(p).wait()
     for j in range(chunks):
         e_copy(j).wait()
 
@@ -293,7 +292,7 @@
         functools.partial(gather_kernel, cent, nz, mass_scale),
         out_shape=(
             jax.ShapeDtypeStruct((local, total), jnp.bfloat16),
-            jax.ShapeDtypeStruct((nz, 2, 4, block_rows, width), jnp.bfloat16),
+            jax.ShapeDtypeStruct((2, nz, 4, block_rows, width), jnp.bfloat16),
             jax.ShapeDtypeStruct((groups, LANES), jnp.float32),
         ),
         in_specs=[pl.BlockSpec(memory_space=pl.ANY)] * 2,
@@ -306,10 +305,10 @@
             pltpu.VMEM((local, width), jnp.bfloat16),
             pltpu.VMEM((local, total), jnp.float32),
             pltpu.VMEM((local, total), jnp.bfloat16),
-            pltpu.VMEM((nz, 2, 4, block_rows, width), jnp.bfloat16),
+            pltpu.VMEM((2, nz, 4, block_rows, width), jnp.bfloat16),
             pltpu.VMEM((cent, 2 * groups, LANES), jnp.float32),
             pltpu.VMEM((groups, LANES), jnp.float32),
-            pltpu.SemaphoreType.DMA((1 + nz,)),
+            pltpu.SemaphoreType.DMA((3,)),
             pltpu.SemaphoreType.DMA((chunks,)),
             pltpu.SemaphoreType.DMA((chunks,)),
             pltpu.SemaphoreType.DMA((nz,)),
@@ -374,7 +373,8 @@
         fits = (
             dp == 2
             and cent % 8 == 0
-            and vectors.shape[0] * 8 == LANES
+            and vectors.shape[0] % 16 == 0
+            and total % (2 * LANES) == 0
             and total <= 1024
             and centroids.shape[0] % SCORE_ROWS == 0
             and centroids.shape[0] <= 4096

time: 42.9 us -> 44.5 us (1.037)
  Pallas kernels: 42.1 us -> 43.8 us
    pallas_call x1, Pallas kernels: 31.7 us -> 33.4 us  [kernel_form(): pl.pallas_call(functools.partial(gather_kernel, cent, nz, mass_scale), ou...]
where the time goes in v4:
time: 44.5 us; the launch traced here: 44.4 us
  Pallas kernels  43.8 us (98%)
  between operations  0.64 us (1%)
    pallas_call x1, Pallas kernels, kernel_form(): pl.pallas_call(functools.partial(gather_kernel, cent, nz, mass_scale), ou...  33.4 us
    pallas_call x1, Pallas kernels, kernel_form(): pl.pallas_call(update_kernel, out_shape=(jax.ShapeDtypeStruct((local, hal...  10.4 us

profile of v4, /device:TPU:0, one launch (start us, length us, event | category | flops | bytes accessed | tf_op | source)
XLA Modules:
  0.0 44.4 jit_solution(8141480339479242081)
XLA Ops:
  0.6 33.4 %shard_map.41 = (bf16[4096,512]{1,0:T(8,128)(2,1)}, bf16[2,4,4,16,1024]{4,3,2,1,0:T(8,128)(2,1)}, f32[4,128]{1,0:T(4,128)}) custom-call(bf16[16,1024]{1,0:T(8,128)(2,1)} %vec_hbm.1, bf16[4096,1024]{1,0:T(8,128)(2,1)} %cen_other.1), custom_call_target="tpu_custom_call" | custom-call | flops 4294967296 | bytes 12582912 | tf_op jit(solution)/shard_map/pallas_call | solution.py:291
  34.0 10.4 %shard_map.42 = (bf16[4096,512]{1,0:T(8,128)(2,1)}, f32[4,8,128]{2,1,0:T(8,128)}) custom-call(s32[1]{0:T(128)} %bitcast.which, bf16[4096,512]{1,0:T(8,128)(2,1)} %get-tuple-element.7.e_ref, f32[4,128]{1,0:T(4,128)} %get-tuple-element.8.resc_ref, bf16[4096,1024]{1,0:T(8,128)(2,1)} %cen_other.1, bf16[4096,1024]{1,0:T(8,128)(2,1)} %cen_other.1, ...), custom_call_target="tpu_custom_call" | custom-call | flops 4294967296 | bytes 16777216 | tf_op jit(solution)/shard_map/pallas_call | solution.py:337

commit v5 on v3

--- a/solution.py
+++ b/solution.py
@@ -87,7 +87,7 @@
     pl.semaphore_wait(barrier, cent)
 
     def slab(o):
-        return lax.rem(z + nz - o, nz)
+        return lax.rem(jnp.where(z < nz // 2, z + o, z + nz - o), nz)
 
     def remote(piece, send_sem, recv_sem, to):
         return pltpu.make_async_remote_copy(
@@ -99,8 +99,8 @@
     y_peer = (x, (z * 2 + 1 - y) * 2 + c)
 
     def over_z(o):
-        to = (x, (lax.rem(z + o, nz) * 2 + y) * 2 + c)
-        return remote(rows.at[z, c, own], z_send.at[o], z_recv.at[o], to)
+        to = (x, (slab(o) * 2 + y) * 2 + c)
+        return remote(rows.at[z, c, own], z_send.at[o], z_recv.at[z], to)
 
     def over_x(o):
         return remote(rows.at[slab(o), c, own], xy_send.at[0, o], xy_recv.at[0, o], x_peer)
@@ -131,7 +131,7 @@
 
     def z_arrival(o):
         piece = rows.at[slab(o), c, own]
-        return remote(piece, z_send.at[o], z_recv.at[o], y_peer)
+        return remote(piece, z_send.at[o], z_recv.at[slab(o)], y_peer)
 
     def forward(o):
         if o:
@@ -161,8 +161,8 @@
     for o in range(1, nz):
         forward(o)
         pass_on(o - 1)
-    complete(0)
-    complete(1)
+        if o >= nz - 2:
+            complete(o - nz + 2)
 
     def score(p, j, peak):
         if p == 0:

time: 42.9 us -> 42.7 us (level)
  no operation moved by 1% of the time
where the time goes in v5:
time: 42.7 us; the launch traced here: 42.5 us
  Pallas kernels  41.9 us (98%)
  between operations  0.64 us (1%)
    pallas_call x1, Pallas kernels, kernel_form(): pl.pallas_call(functools.partial(gather_kernel, cent, nz, mass_scale), ou...  31.5 us
    pallas_call x1, Pallas kernels, kernel_form(): pl.pallas_call(update_kernel, out_shape=(jax.ShapeDtypeStruct((local, hal...  10.4 us

profile of v5, /device:TPU:0, one launch (start us, length us, event | category | flops | bytes accessed | tf_op | source)
XLA Modules:
  0.0 42.5 jit_solution(15133943098824714136)
XLA Ops:
  0.6 31.5 %shard_map.41 = (bf16[4096,512]{1,0:T(8,128)(2,1)}, bf16[4,2,4,16,1024]{4,3,2,1,0:T(8,128)(2,1)}, f32[4,128]{1,0:T(4,128)}) custom-call(bf16[16,1024]{1,0:T(8,128)(2,1)} %vec_hbm.1, bf16[4096,1024]{1,0:T(8,128)(2,1)} %cen_other.1), custom_call_target="tpu_custom_call" | custom-call | flops 4294967296 | bytes 12582912 | tf_op jit(solution)/shard_map/pallas_call | solution.py:292
  32.1 10.4 %shard_map.42 = (bf16[4096,512]{1,0:T(8,128)(2,1)}, f32[4,8,128]{2,1,0:T(8,128)}) custom-call(s32[1]{0:T(128)} %bitcast.which, bf16[4096,512]{1,0:T(8,128)(2,1)} %get-tuple-element.7.e_ref, f32[4,128]{1,0:T(4,128)} %get-tuple-element.8.resc_ref, bf16[4096,1024]{1,0:T(8,128)(2,1)} %cen_other.1, bf16[4096,1024]{1,0:T(8,128)(2,1)} %cen_other.1, ...), custom_call_target="tpu_custom_call" | custom-call | flops 4294967296 | bytes 16777216 | tf_op jit(solution)/shard_map/pallas_call | solution.py:338

commit v6 on v5

--- a/solution.py
+++ b/solution.py
@@ -12,6 +12,7 @@
 LANES = 128
 SCORE_ROWS = 1024
 SUM_ROWS = 1024
+PIECE_ROWS = 512
 EXP_ROWS = 64
 VMEM_BYTES = 56 * 1024 * 1024
 
@@ -255,28 +256,32 @@
 ):
     j = pl.program_id(0)
     groups = resc_ref.shape[0]
-    mass = None
-    parts = []
-    for g in range(groups):
-        lanes = slice(g * LANES, (g + 1) * LANES)
-        p = e_ref[:, lanes].astype(jnp.float32) * resc_ref[g : g + 1, :]
-        mass = p if mass is None else mass + p
-        parts.append(p.astype(jnp.bfloat16))
-    weights = jnp.concatenate(parts, axis=1)
-    for b in range(mass.shape[0] // LANES):
-        block = mass[b * LANES : (b + 1) * LANES].T
-        loads_ref[j, b : b + 1, :] = jnp.sum(block, axis=0, keepdims=True)
-    own = cen_own[...].astype(jnp.float32) + jnp.dot(
-        weights, rows_own[...], preferred_element_type=jnp.float32
-    )
-    other = cen_other[...].astype(jnp.float32) + jnp.dot(
-        weights, rows_other[...], preferred_element_type=jnp.float32
-    )
-    width = own.shape[1] + other.shape[1]
-    square = (
-        jnp.sum(own * own, axis=1, keepdims=True) + jnp.sum(other * other, axis=1, keepdims=True)
-    ) / width
-    new_ref[...] = (own * lax.rsqrt(square + 1e-06)).astype(new_ref.dtype)
+    width = cen_own.shape[1] + cen_other.shape[1]
+    for start in range(0, SUM_ROWS, PIECE_ROWS):
+        span = slice(start, start + PIECE_ROWS)
+        mass = None
+        parts = []
+        for g in range(groups):
+            lanes = slice(g * LANES, (g + 1) * LANES)
+            p = e_ref[span, lanes].astype(jnp.float32) * resc_ref[g : g + 1, :]
+            mass = p if mass is None else mass + p
+            parts.append(p.astype(jnp.bfloat16))
+        weights = jnp.concatenate(parts, axis=1)
+        for b in range(PIECE_ROWS // LANES):
+            block = mass[b * LANES : (b + 1) * LANES].T
+            at = start // LANES + b
+            loads_ref[j, at : at + 1, :] = jnp.sum(block, axis=0, keepdims=True)
+        own = cen_own[span].astype(jnp.float32) + jnp.dot(
+            weights, rows_own[...], preferred_element_type=jnp.float32
+        )
+        other = cen_other[span].astype(jnp.float32) + jnp.dot(
+            weights, rows_other[...], preferred_element_type=jnp.float32
+        )
+        square = (
+            jnp.sum(own * own, axis=1, keepdims=True)
+            + jnp.sum(other * other, axis=1, keepdims=True)
+        ) / width
+        new_ref[span] = (own * lax.rsqrt(square + 1e-06)).astype(new_ref.dtype)
 
 
 def kernel_form(vectors, centroids):

time: 42.7 us -> 42.6 us (level)
  no operation moved by 1% of the time
where the time goes in v6:
time: 42.6 us; the launch traced here: 42.5 us
  Pallas kernels  41.9 us (98%)
  between operations  0.64 us (2%)
    pallas_call x1, Pallas kernels, kernel_form(): pl.pallas_call(functools.partial(gather_kernel, cent, nz, mass_scale), ou...  31.5 us
    pallas_call x1, Pallas kernels, kernel_form(): pl.pallas_call(update_kernel, out_shape=(jax.ShapeDtypeStruct((local, hal...  10.3 us

profile of v6, /device:TPU:0, one launch (start us, length us, event | category | flops | bytes accessed | tf_op | source)
XLA Modules:
  0.0 42.5 jit_solution(7858840834363074523)
XLA Ops:
  0.6 31.5 %shard_map.41 = (bf16[4096,512]{1,0:T(8,128)(2,1)}, bf16[4,2,4,16,1024]{4,3,2,1,0:T(8,128)(2,1)}, f32[4,128]{1,0:T(4,128)}) custom-call(bf16[16,1024]{1,0:T(8,128)(2,1)} %vec_hbm.1, bf16[4096,1024]{1,0:T(8,128)(2,1)} %cen_other.1), custom_call_target="tpu_custom_call" | custom-call | flops 4294967296 | bytes 12582912 | tf_op jit(solution)/shard_map/pallas_call | solution.py:297
  32.1 10.3 %shard_map.42 = (bf16[4096,512]{1,0:T(8,128)(2,1)}, f32[4,8,128]{2,1,0:T(8,128)}) custom-call(s32[1]{0:T(128)} %bitcast.which, bf16[4096,512]{1,0:T(8,128)(2,1)} %get-tuple-element.7.e_ref, f32[4,128]{1,0:T(4,128)} %get-tuple-element.8.resc_ref, bf16[4096,1024]{1,0:T(8,128)(2,1)} %cen_other.1, bf16[4096,1024]{1,0:T(8,128)(2,1)} %cen_other.1, ...), custom_call_target="tpu_custom_call" | custom-call | flops 4294967296 | bytes 16777216 | tf_op jit(solution)/shard_map/pallas_call | solution.py:343
